TPU v7x, 32 devices: a whole 2x2x4 slice. The times are simulated.
32 devices in a mesh: op: 4 (over y, x), sec: 8 (over z, core).
Axes of the slice: x: 2, y: 2, z: 4, core: 2. Of those that a mesh axis runs over, the one named last changes fastest.
Arguments:
- wavefunction: bfloat16 [512, 128, 128], P('sec'), may hold values from -6 to 6
- left_ops: bfloat16 [2, 16, 8, 128, 128], P(None, 'op'), may hold values from -0.5 to 0.5
- right_ops: bfloat16 [2, 16, 8, 128, 128], P(None, 'op'), may hold values from -0.09375 to 0.09375
- left_sector: int32 [512], P('sec'), may hold values from 0 to 7
- right_sector: int32 [512], P('sec'), may hold values from 0 to 7
- target: int32 [2, 512], replicated, may hold values from 0 to 511, as said below
Outputs:
- applied_blocks: float32 [512, 128, 128], P('sec', 'op')
Inputs may be any that keep to these rules, and one draw needn't show every extreme that they name: For every class, target is a permutation of the 512 blocks; block b lies on index b // 64 of sec, and for every class exactly 8 of the blocks of one index of sec map to blocks of each index of sec.
All inputs are finite; a program needn't handle non-finite values.
Results may differ from a plain program's by a relative error of at most 0.0029.
Values may be sent and summed in bfloat16 or wider, within the bound.
A program may use at most 64 MiB of HBM per device.

v0:
```python
import jax
import jax.numpy as jnp
from jax import lax
from jax.sharding import PartitionSpec as P


def class_terms(initial, left_ops, right_ops, wavefunction, left_sector, right_sector):

    def add_term(running, operators):
        left_term, right_term = operators
        left_blocks = jnp.take(left_term, left_sector, axis=0)
        left_mixed = jnp.einsum(
            "bij,bjk->bik", left_blocks, wavefunction, preferred_element_type=jnp.float32
        ).astype(jnp.bfloat16)
        right_blocks = jnp.take(right_term, right_sector, axis=0)
        return (
            running
            + jnp.einsum(
                "bik,blk->bil", left_mixed, right_blocks, preferred_element_type=jnp.float32
            ),
            None,
        )

    running, _ = lax.scan(add_term, initial, (left_ops, right_ops))
    return running


def routing(target_row, blocks_here, own_index, shards):
    slots = blocks_here // shards
    dest_device = (target_row // blocks_here).reshape(shards, blocks_here)
    dest_slot = (target_row % blocks_here).reshape(shards, blocks_here)
    slot_ids = jnp.arange(blocks_here, dtype=jnp.int32)
    same_dest = dest_device[:, :, None] == dest_device[:, None, :]
    earlier = slot_ids[None, :] < slot_ids[:, None]
    rank_in = jnp.sum((same_dest & earlier[None, :, :]).astype(jnp.int32), axis=2)
    position = dest_device * slots + rank_in
    own_position = lax.dynamic_index_in_dim(position, own_index, 0, keepdims=False)
    send_index = jnp.sum(
        jnp.where(own_position[None, :] == slot_ids[:, None], slot_ids[None, :], 0), axis=1
    )
    source = jnp.arange(shards, dtype=jnp.int32)[:, None]
    arrival = source * slots + rank_in
    for_here = dest_device == own_index
    arrives_here = for_here[:, :, None] & (dest_slot[:, :, None] == slot_ids[None, None, :])
    recv_index = jnp.sum(jnp.where(arrives_here, arrival[:, :, None], 0), axis=(0, 1))
    return (send_index, recv_index)


def per_device(wavefunction, left_ops, right_ops, left_sector, right_sector, target):
    shards = lax.axis_size("sec")
    own_index = lax.axis_index("sec")
    blocks_here = wavefunction.shape[0]
    classes = target.shape[0]
    empty = jnp.zeros(wavefunction.shape, jnp.float32)
    gathered_sum = None
    for class_index in range(classes):
        summed = class_terms(
            empty,
            left_ops[class_index],
            right_ops[class_index],
            wavefunction,
            left_sector,
            right_sector,
        )
        send_index, recv_index = routing(target[class_index], blocks_here, own_index, shards)
        share = lax.psum_scatter(summed, "op", scatter_dimension=1, tiled=True)
        arrived = lax.all_to_all(
            jnp.take(share, send_index, axis=0), "sec", split_axis=0, concat_axis=0, tiled=True
        )
        placed = jnp.take(arrived, recv_index, axis=0)
        gathered_sum = placed if gathered_sum is None else gathered_sum + placed
    return gathered_sum


def solution(mesh):
    in_specs = (
        P("sec", None, None),
        P(None, "op", None, None, None),
        P(None, "op", None, None, None),
        P("sec"),
        P("sec"),
        P(),
    )
    out_specs = P("sec", "op", None)
    return jax.shard_map(
        per_device, mesh=mesh, in_specs=in_specs, out_specs=out_specs, check_vma=False
    )
```

profile of v0, /device:TPU:0, one launch (start us, length us, event | category | flops | bytes accessed | tf_op | source)
XLA Modules:
  0.0 211.4 jit_solution(13783630016928985739)
XLA Ops:
  6.5 4.4 %slice_bitcast_fusion.2 = (bf16[4,8,128,128]{3,2,1,0:T(8,128)(2,1)}, bf16[4,8,128,128]{3,2,1,0:T(8,128)(2,1)}, bf16[4,8,128,128]{3,2,1,0:T(8,128)(2,1)}, bf16[4,8,128,128]{3,2,1,0:T(8,128)(2,1)}) fusion(bf16[2,4,8,128,128]{4,3,2,1,0:T(8,128)(2,1)} %param.16, bf16[2,4,8,128,128]{4,3,2,1,0:T(8,128)(2,1)} %param.15), kind=kLoop, calls=%fused_computation.45 | loop fusion | bytes 8388608 | tf_op jit(solution)/shard_map/squeeze | solution.py:60
  10.9 46.2 %while.23 = (s32[]{:T(128)}, f32[64,128,128]{2,1,0:T(8,128)}, bf16[4,8,128,128]{3,2,1,0:T(8,128)(2,1)}, s32[64]{0:T(128)S(1)}, bf16[64,128,128]{2,1,0:T(8,128)(2...) while((s32[]{:T(128)}, f32[64,128,128]{2,1,0:T(8,128)}, ...), condition=%wide.region_7.10_spmd.clone, body=%wide.region_6.9_spmd.clone.sunk | while | flops 542116992 | bytes 24128372 | solution.py:24
  13.0 2.1 %gather_fusion.3 = bf16[64,128,128]{2,1,0:T(8,128)(2,1)} fusion(bf16[8,128,128]{2,1,0:T(8,128)(2,1)S(1)} %get-tuple-element.302, s32[1024]{0:T(1024)S(1)} %pad_clamp_fusion.15), kind=kCustom, calls=%fused_computation.3.clone.clone.1 | custom fusion | bytes 4194560 | tf_op jit(solution)/shard_map/while/body/eval_jaxpr/jit(_take)/gather | solution.py:11
  15.2 6.4 %select_add_fusion.6 = f32[64,128,128]{2,1,0:T(8,128)} fusion(f32[64,128,128]{2,1,0:T(8,128)} %get-tuple-element.315, bf16[64,128,128]{2,1,0:T(8,128)(2,1)S(1)} %gather_fusion.2, pred[64]{0:T(512)(128)(4,1)S(1)} %get-tuple-element.301, pred[]{:T(512)S(6)} %compare.51, bf16[64,128,128]{2,1,0:T(8,128)(2,1)} %get-tuple-element.327, ...), kind=kOutput, calls=%fused_computation.25.clone.1 | convolution fusion | flops 542113792 | bytes 14680193 | tf_op jit(solution)/shard_map/while/body/eval_jaxpr/bik,blk->bil/dot_general | solution.py:18
  23.7 2.1 %gather_fusion.3 = bf16[64,128,128]{2,1,0:T(8,128)(2,1)} fusion(bf16[8,128,128]{2,1,0:T(8,128)(2,1)S(1)} %get-tuple-element.302, s32[1024]{0:T(1024)S(1)} %pad_clamp_fusion.15), kind=kCustom, calls=%fused_computation.3.clone.clone.1 | custom fusion | bytes 4194560 | tf_op jit(solution)/shard_map/while/body/eval_jaxpr/jit(_take)/gather | solution.py:11
  25.8 7.6 %select_add_fusion.6 = f32[64,128,128]{2,1,0:T(8,128)} fusion(f32[64,128,128]{2,1,0:T(8,128)} %get-tuple-element.315, bf16[64,128,128]{2,1,0:T(8,128)(2,1)S(1)} %gather_fusion.2, pred[64]{0:T(512)(128)(4,1)S(1)} %get-tuple-element.301, pred[]{:T(512)S(6)} %compare.51, bf16[64,128,128]{2,1,0:T(8,128)(2,1)} %get-tuple-element.327, ...), kind=kOutput, calls=%fused_computation.25.clone.1 | convolution fusion | flops 542113792 | bytes 14680193 | tf_op jit(solution)/shard_map/while/body/eval_jaxpr/bik,blk->bil/dot_general | solution.py:18
  35.5 2.1 %gather_fusion.3 = bf16[64,128,128]{2,1,0:T(8,128)(2,1)} fusion(bf16[8,128,128]{2,1,0:T(8,128)(2,1)S(1)} %get-tuple-element.302, s32[1024]{0:T(1024)S(1)} %pad_clamp_fusion.15), kind=kCustom, calls=%fused_computation.3.clone.clone.1 | custom fusion | bytes 4194560 | tf_op jit(solution)/shard_map/while/body/eval_jaxpr/jit(_take)/gather | solution.py:11
  37.7 7.6 %select_add_fusion.6 = f32[64,128,128]{2,1,0:T(8,128)} fusion(f32[64,128,128]{2,1,0:T(8,128)} %get-tuple-element.315, bf16[64,128,128]{2,1,0:T(8,128)(2,1)S(1)} %gather_fusion.2, pred[64]{0:T(512)(128)(4,1)S(1)} %get-tuple-element.301, pred[]{:T(512)S(6)} %compare.51, bf16[64,128,128]{2,1,0:T(8,128)(2,1)} %get-tuple-element.327, ...), kind=kOutput, calls=%fused_computation.25.clone.1 | convolution fusion | flops 542113792 | bytes 14680193 | tf_op jit(solution)/shard_map/while/body/eval_jaxpr/bik,blk->bil/dot_general | solution.py:18
  47.4 2.1 %gather_fusion.3 = bf16[64,128,128]{2,1,0:T(8,128)(2,1)} fusion(bf16[8,128,128]{2,1,0:T(8,128)(2,1)S(1)} %get-tuple-element.302, s32[1024]{0:T(1024)S(1)} %pad_clamp_fusion.15), kind=kCustom, calls=%fused_computation.3.clone.clone.1 | custom fusion | bytes 4194560 | tf_op jit(solution)/shard_map/while/body/eval_jaxpr/jit(_take)/gather | solution.py:11
  49.5 7.6 %select_add_fusion.6 = f32[64,128,128]{2,1,0:T(8,128)} fusion(f32[64,128,128]{2,1,0:T(8,128)} %get-tuple-element.315, bf16[64,128,128]{2,1,0:T(8,128)(2,1)S(1)} %gather_fusion.2, pred[64]{0:T(512)(128)(4,1)S(1)} %get-tuple-element.301, pred[]{:T(512)S(6)} %compare.51, bf16[64,128,128]{2,1,0:T(8,128)(2,1)} %get-tuple-element.327, ...), kind=kOutput, calls=%fused_computation.25.clone.1 | convolution fusion | flops 542113792 | bytes 14680193 | tf_op jit(solution)/shard_map/while/body/eval_jaxpr/bik,blk->bil/dot_general | solution.py:18
  57.2 47.7 %while.22 = (s32[]{:T(128)}, f32[64,128,128]{2,1,0:T(8,128)}, bf16[4,8,128,128]{3,2,1,0:T(8,128)(2,1)}, s32[64]{0:T(128)S(1)}, bf16[64,128,128]{2,1,0:T(8,128)(2...) while((s32[]{:T(128)}, f32[64,128,128]{2,1,0:T(8,128)}, ...), condition=%wide.region_1.0_spmd.clone, body=%wide.region_0.2_spmd.clone.sunk | while | flops 542116992 | bytes 24128372 | solution.py:24
  59.3 2.2 %gather_fusion.1 = bf16[64,128,128]{2,1,0:T(8,128)(2,1)} fusion(bf16[8,128,128]{2,1,0:T(8,128)(2,1)S(1)} %get-tuple-element.289, s32[1024]{0:T(1024)S(1)} %pad_clamp_fusion.13), kind=kCustom, calls=%fused_computation.clone.clone.1 | custom fusion | bytes 4194560 | tf_op jit(solution)/shard_map/while/body/eval_jaxpr/jit(_take)/gather | solution.py:11
  61.5 6.4 %select_add_fusion.5 = f32[64,128,128]{2,1,0:T(8,128)} fusion(f32[64,128,128]{2,1,0:T(8,128)} %get-tuple-element.342, bf16[64,128,128]{2,1,0:T(8,128)(2,1)S(1)} %gather_fusion, pred[64]{0:T(512)(128)(4,1)S(1)} %get-tuple-element.288, pred[]{:T(512)S(6)} %compare.50, bf16[64,128,128]{2,1,0:T(8,128)(2,1)} %get-tuple-element.354, ...), kind=kOutput, calls=%fused_computation.8.clone.1 | convolution fusion | flops 542113792 | bytes 14680193 | tf_op jit(solution)/shard_map/while/body/eval_jaxpr/bik,blk->bil/dot_general | solution.py:18
  70.0 2.2 %gather_fusion.1 = bf16[64,128,128]{2,1,0:T(8,128)(2,1)} fusion(bf16[8,128,128]{2,1,0:T(8,128)(2,1)S(1)} %get-tuple-element.289, s32[1024]{0:T(1024)S(1)} %pad_clamp_fusion.13), kind=kCustom, calls=%fused_computation.clone.clone.1 | custom fusion | bytes 4194560 | tf_op jit(solution)/shard_map/while/body/eval_jaxpr/jit(_take)/gather | solution.py:11
  72.3 7.9 %select_add_fusion.5 = f32[64,128,128]{2,1,0:T(8,128)} fusion(f32[64,128,128]{2,1,0:T(8,128)} %get-tuple-element.342, bf16[64,128,128]{2,1,0:T(8,128)(2,1)S(1)} %gather_fusion, pred[64]{0:T(512)(128)(4,1)S(1)} %get-tuple-element.288, pred[]{:T(512)S(6)} %compare.50, bf16[64,128,128]{2,1,0:T(8,128)(2,1)} %get-tuple-element.354, ...), kind=kOutput, calls=%fused_computation.8.clone.1 | convolution fusion | flops 542113792 | bytes 14680193 | tf_op jit(solution)/shard_map/while/body/eval_jaxpr/bik,blk->bil/dot_general | solution.py:18
  82.3 2.2 %gather_fusion.1 = bf16[64,128,128]{2,1,0:T(8,128)(2,1)} fusion(bf16[8,128,128]{2,1,0:T(8,128)(2,1)S(1)} %get-tuple-element.289, s32[1024]{0:T(1024)S(1)} %pad_clamp_fusion.13), kind=kCustom, calls=%fused_computation.clone.clone.1 | custom fusion | bytes 4194560 | tf_op jit(solution)/shard_map/while/body/eval_jaxpr/jit(_take)/gather | solution.py:11
  84.5 7.8 %select_add_fusion.5 = f32[64,128,128]{2,1,0:T(8,128)} fusion(f32[64,128,128]{2,1,0:T(8,128)} %get-tuple-element.342, bf16[64,128,128]{2,1,0:T(8,128)(2,1)S(1)} %gather_fusion, pred[64]{0:T(512)(128)(4,1)S(1)} %get-tuple-element.288, pred[]{:T(512)S(6)} %compare.50, bf16[64,128,128]{2,1,0:T(8,128)(2,1)} %get-tuple-element.354, ...), kind=kOutput, calls=%fused_computation.8.clone.1 | convolution fusion | flops 542113792 | bytes 14680193 | tf_op jit(solution)/shard_map/while/body/eval_jaxpr/bik,blk->bil/dot_general | solution.py:18
  94.3 2.2 %gather_fusion.1 = bf16[64,128,128]{2,1,0:T(8,128)(2,1)} fusion(bf16[8,128,128]{2,1,0:T(8,128)(2,1)S(1)} %get-tuple-element.289, s32[1024]{0:T(1024)S(1)} %pad_clamp_fusion.13), kind=kCustom, calls=%fused_computation.clone.clone.1 | custom fusion | bytes 4194560 | tf_op jit(solution)/shard_map/while/body/eval_jaxpr/jit(_take)/gather | solution.py:11
  96.5 8.4 %select_add_fusion.5 = f32[64,128,128]{2,1,0:T(8,128)} fusion(f32[64,128,128]{2,1,0:T(8,128)} %get-tuple-element.342, bf16[64,128,128]{2,1,0:T(8,128)(2,1)S(1)} %gather_fusion, pred[64]{0:T(512)(128)(4,1)S(1)} %get-tuple-element.288, pred[]{:T(512)S(6)} %compare.50, bf16[64,128,128]{2,1,0:T(8,128)(2,1)} %get-tuple-element.354, ...), kind=kOutput, calls=%fused_computation.8.clone.1 | convolution fusion | flops 542113792 | bytes 14680193 | tf_op jit(solution)/shard_map/while/body/eval_jaxpr/bik,blk->bil/dot_general | solution.py:18
  106.6 6.1 %reduce-scatter.5.cloned.1.call-done = f32[64,32,128]{2,1,0:T(8,128)} async-done(((f32[64,128,128]{2,1,0:T(8,128)}), f32[64,32,128]{2,1,0:T(8,128)}) %reduce-scatter.5.cloned.1.call-update) | async-done | bytes 1048592 | tf_op jit(solution)/shard_map/reduce_scatter | solution.py:66
  115.6 4.6 %all-to-all-start.1 = ((f32[64,32,128]{2,1,0:T(8,128)}), f32[64,32,128]{2,1,0:T(8,128)S(1)}, u32[]{:S(2)}, u32[]{:S(2)}) async-start(f32[64,32,128]{2,1,0:T(8,128)} %broadcast_select_fusion), calls=%async_computation.3 | async-start | bytes 2097152 | tf_op jit(solution)/shard_map/all_to_all | solution.py:67
  120.4 48.2 %reduce-scatter.3.cloned.1.call-done = f32[64,32,128]{2,1,0:T(8,128)} async-done(((f32[64,128,128]{2,1,0:T(8,128)}), f32[64,32,128]{2,1,0:T(8,128)}) %reduce-scatter.3.cloned.1.call-update) | async-done | bytes 1048592 | tf_op jit(solution)/shard_map/reduce_scatter | solution.py:66
  171.6 4.6 %all-to-all-start = ((f32[64,32,128]{2,1,0:T(8,128)}), f32[64,32,128]{2,1,0:T(8,128)S(1)}, u32[]{:S(2)}, u32[]{:S(2)}) async-start(f32[64,32,128]{2,1,0:T(8,128)} %broadcast_select_fusion.1), calls=%async_computation.1 | async-start | bytes 2097152 | tf_op jit(solution)/shard_map/all_to_all | solution.py:67
  177.5 25.3 %all-to-all-done = f32[64,32,128]{2,1,0:T(8,128)S(1)} async-done(((f32[64,32,128]{2,1,0:T(8,128)}), f32[64,32,128]{2,1,0:T(8,128)S(1)}, u32[]{:S(2)}, u32[]{:S(2)}) %all-to-all-start) | async-done | bytes 1048608 | tf_op jit(solution)/shard_map/all_to_all | solution.py:67
  (95 shorter events, 27.1 us)
Async XLA Ops:
  6.5 106.2 %reduce-scatter.5.cloned.1.call-start = ((), (), s32[]{:S(2)}) async-start(), calls=%async_computation.5 | async-start | bytes 5242880 | tf_op jit(solution)/shard_map/reduce_scatter | solution.py:66
  6.5 4.4 %copy-start = (s32[64]{0:T(128)S(1)}, s32[64]{0:T(128)}, u32[]{:S(2)}) copy-start(s32[64]{0:T(128)} %param.17) | copy-start | bytes 772
  6.5 4.4 %copy-start.1 = (s32[64]{0:T(128)S(1)}, s32[64]{0:T(128)}, u32[]{:S(2)}) copy-start(s32[64]{0:T(128)} %param.18) | copy-start | bytes 772
  57.2 111.4 %reduce-scatter.3.cloned.1.call-start = ((), (), s32[]{:S(2)}) async-start(), calls=%async_computation.4 | async-start | bytes 5242880 | tf_op jit(solution)/shard_map/reduce_scatter | solution.py:66
  104.9 0.7 copy-start.2
  115.6 55.9 %all-to-all-start.1 = ((f32[64,32,128]{2,1,0:T(8,128)}), f32[64,32,128]{2,1,0:T(8,128)S(1)}, u32[]{:S(2)}, u32[]{:S(2)}) async-start(f32[64,32,128]{2,1,0:T(8,128)} %broadcast_select_fusion), calls=%async_computation.3 | async-start | bytes 2097152 | tf_op jit(solution)/shard_map/all_to_all | solution.py:67
  171.6 31.2 %all-to-all-start = ((f32[64,32,128]{2,1,0:T(8,128)}), f32[64,32,128]{2,1,0:T(8,128)S(1)}, u32[]{:S(2)}, u32[]{:S(2)}) async-start(f32[64,32,128]{2,1,0:T(8,128)} %broadcast_select_fusion.1), calls=%async_computation.1 | async-start | bytes 2097152 | tf_op jit(solution)/shard_map/all_to_all | solution.py:67
Sparse Core Ops, SparseCore 0:
  57.3 55.3 reduce-scatter.4
  115.9 52.6 reduce-scatter.2
where the time goes:
time: 212 us; the launch traced here: 211 us
  waiting for transfers between devices  79.7 us (38%)
  matrix products  59.7 us (28%)
  local copies, waits for them, and re-layouts  43.7 us (21%)
  between operations  13.6 us (6%)
  starting transfers between devices  9.25 us (4%)
  other arithmetic  5.14 us (2%)
    dot_general x8, matrix products, add_term(): jnp.einsum('bik,blk->bil', left_mixed, right_blocks, preferred_element_ty...  59.7 us
    reduce_scatter x2, waiting for transfers between devices, per_device(): share = lax.psum_scatter(summed, 'op', scatter_dimension=1, tiled=True)  54.3 us
    all_to_all x2, waiting for transfers between devices, per_device(): lax.all_to_all(jnp.take(share, send_index, axis=0), 'sec', split_axis=0,...  25.3 us
    gather x8, local copies, waits for them, and re-layouts, add_term(): left_blocks = jnp.take(left_term, left_sector, axis=0)  17.4 us
    all_to_all x2, starting transfers between devices, per_device(): lax.all_to_all(jnp.take(share, send_index, axis=0), 'sec', split_axis=0,...  9.21 us
    squeeze x8, local copies, waits for them, and re-layouts, class_terms(): running, _ = lax.scan(add_term, initial, (left_ops, right_ops))  8.53 us
    gather x8, local copies, waits for them, and re-layouts, add_term(): right_blocks = jnp.take(right_term, right_sector, axis=0)  7.61 us
    squeeze x1, local copies, waits for them, and re-layouts, per_device(): right_ops[class_index]  4.39 us
  transfers between devices with their start and end apart: 4, of which 3 were waited for; matrix products, arithmetic and copies ran while one was open for 26% of the time, Pallas kernels for 0%

commit v1 on v0

v1 whole, which is shorter than its diff:
```python
import functools

import jax
import jax.numpy as jnp
from jax import lax
from jax.experimental import pallas as pl
from jax.experimental.pallas import tpu as pltpu
from jax.sharding import PartitionSpec as P

MESH = pl.DeviceIdType.MESH
GROUP = 8
LAG_SECOND = 1
LAG_ROUTE = 2


def kernel(sizes, left_sm, right_sm, send_sm, recv_sm, w_ref, l_ref, r_ref, out_ref,
           acc, s1, r1, s2, r2, s3, arr, sem_s1, sem_r1, sem_s2, sem_r2, sem_s3, sem_r3):
    shards, classes, chunks, chunk, slots = sizes
    half = chunk // 2
    terms, bl = l_ref.shape[1], l_ref.shape[3]
    rows = acc.shape[3]
    op, me = lax.axis_index("op"), lax.axis_index("sec")
    hi, lo = op // 2, op % 2
    own = hi * 2 + lo
    near_lo, near_hi = hi * 2 + 1 - lo, (1 - hi) * 2 + lo
    dests = chunk // slots

    def peer(k):
        off = shards // 2 + (1 - 2 * (k % 2)) * ((k + 1) // 2)
        return (me + off + shards) % shards

    barrier = pltpu.get_barrier_semaphore()
    for other in (near_lo, near_hi):
        pl.semaphore_signal(barrier, inc=1, device_id={"op": other}, device_id_type=MESH)

    def greet(k, carry):
        pl.semaphore_signal(barrier, inc=1, device_id={"sec": peer(k)}, device_id_type=MESH)
        return carry

    lax.fori_loop(0, shards - 1, greet, 0)
    pl.semaphore_wait(barrier, 2 + shards - 1)

    def first_copy(h, i):
        return pltpu.make_async_remote_copy(
            src_ref=s1.at[h, i], dst_ref=r1.at[h, i], send_sem=sem_s1.at[h, i], recv_sem=sem_r1.at[h, i],
            device_id={"op": near_lo if h == 0 else near_hi}, device_id_type=MESH)

    def second_copy(h, i):
        return pltpu.make_async_remote_copy(
            src_ref=s2.at[h, i], dst_ref=r2.at[h, i], send_sem=sem_s2.at[h, i], recv_sem=sem_r2.at[h, i],
            device_id={"op": near_hi if h == 0 else near_lo}, device_id_type=MESH)

    def route_copy(i, e, q, k):
        return pltpu.make_async_remote_copy(
            src_ref=s3.at[i, e], dst_ref=arr.at[q, me], send_sem=sem_s3.at[i, e], recv_sem=sem_r3.at[q, me],
            device_id={"sec": peer(k)}, device_id_type=MESH)

    def compute(i):
        q, c = i % classes, i // classes
        for b in range(chunk):
            dest = peer(c * dests + b // slots)
            block = send_sm[q, dest * slots + b % slots]
            left = left_sm[block]
            right = right_sm[block]
            mixed = jnp.dot(
                l_ref[q, :, left].reshape(terms * bl, l_ref.shape[4]), w_ref[block],
                preferred_element_type=jnp.float32).astype(jnp.bfloat16)
            mixed = jnp.concatenate([mixed[t * bl:(t + 1) * bl] for t in range(terms)], axis=1)
            rights = jnp.concatenate([r_ref[q, t, right] for t in range(terms)], axis=1)
            value = lax.dot_general(mixed, rights, (((1,), (1,)), ((), ())), preferred_element_type=jnp.float32)
            acc[i, b] = value.reshape(acc.shape[2:])
        for j in range(2):
            s1[0, i, :, j] = acc[i, 0:half, j * 2 + 1 - lo].astype(jnp.bfloat16)
        first_copy(0, i).start()
        for j in range(2):
            s1[1, i, :, j] = acc[i, half:chunk, (1 - hi) * 2 + j].astype(jnp.bfloat16)
        first_copy(1, i).start()

    def second(i):
        first_copy(0, i).wait_recv()
        s2[0, i] = (acc[i, 0:half, near_hi] + r1[0, i, :, 1 - hi].astype(jnp.float32)).astype(jnp.bfloat16)
        second_copy(0, i).start()
        first_copy(1, i).wait_recv()
        s2[1, i] = (acc[i, half:chunk, near_lo] + r1[1, i, :, 1 - lo].astype(jnp.float32)).astype(jnp.bfloat16)
        second_copy(1, i).start()
        acc[i, 0:half, own] = acc[i, 0:half, own] + r1[0, i, :, hi].astype(jnp.float32)
        acc[i, half:chunk, own] = acc[i, half:chunk, own] + r1[1, i, :, lo].astype(jnp.float32)

    def route(i):
        q, c = i % classes, i // classes
        for h in range(2):
            second_copy(h, i).wait_recv()
            total = acc[i, h * half:(h + 1) * half, own] + r2[h, i].astype(jnp.float32)
            acc[i, h * half:(h + 1) * half, own] = total
        for e in range(dests):
            k = c * dests + e
            share = acc[i, e * slots:(e + 1) * slots, own].astype(jnp.bfloat16)

            @pl.when(k < shards - 1)
            def _():
                s3[i, e] = share
                route_copy(i, e, q, k).start()

            @pl.when(k == shards - 1)
            def _():
                arr[q, me] = share

    def step(i, carry):
        @pl.when(i < chunks)
        def _():
            compute(i)

        @pl.when((i >= LAG_SECOND) & (i < chunks + LAG_SECOND))
        def _():
            second(i - LAG_SECOND)

        @pl.when(i >= LAG_ROUTE)
        def _():
            route(i - LAG_ROUTE)

        return carry

    lax.fori_loop(0, chunks + LAG_ROUTE, step, 0)

    def arrive(k, carry):
        source = peer(k)
        for q in range(classes):
            pltpu.make_async_remote_copy(
                src_ref=s3.at[0, 0], dst_ref=arr.at[q, source], send_sem=sem_s3.at[0, 0],
                recv_sem=sem_r3.at[q, source], device_id={"sec": source}, device_id_type=MESH).wait_recv()
        return carry

    lax.fori_loop(0, shards - 1, arrive, 0)

    def place(n, carry):
        for u in range(GROUP):
            slot = n * GROUP + u
            total = None
            for q in range(classes):
                at = recv_sm[q, slot]
                here = arr[q, at // slots, at % slots].astype(jnp.float32)
                total = here if total is None else total + here
            out_ref[slot] = total
        return carry

    lax.fori_loop(0, out_ref.shape[0] // GROUP, place, 0)

    def drain(i, carry):
        for h in range(2):
            first_copy(h, i).wait_send()
            second_copy(h, i).wait_send()
        for e in range(dests):
            k = (i // classes) * dests + e

            @pl.when(k < shards - 1)
            def _():
                route_copy(i, e, i % classes, k).wait_send()
        return carry

    lax.fori_loop(0, chunks, drain, 0)


def routing(target, blocks_here, own_index, shards):
    slots = blocks_here // shards
    slot_ids = jnp.arange(blocks_here, dtype=jnp.int32)
    mine = lax.dynamic_slice_in_dim(target, own_index * blocks_here, blocks_here, 1)
    position = jnp.sum((mine[:, None, :] < mine[:, :, None]).astype(jnp.int32), axis=2)
    send_index = jnp.sum(jnp.where(position[:, None, :] == slot_ids[:, None], slot_ids, 0), axis=2)
    wanted = own_index * blocks_here + slot_ids
    devices = jnp.arange(target.shape[1], dtype=jnp.int32) // blocks_here
    source = jnp.sum(jnp.where(target[:, None, :] == wanted[:, None], devices, 0), axis=2)
    same = (source[:, None, :] == source[:, :, None]) & (slot_ids[None, :] < slot_ids[:, None])
    recv_index = source * slots + jnp.sum(same.astype(jnp.int32), axis=2)
    return send_index, recv_index


def per_device(wavefunction, left_ops, right_ops, left_sector, right_sector, target):
    shards, parts = lax.axis_size("sec"), lax.axis_size("op")
    assert parts == 4
    blocks_here, bl, br = wavefunction.shape
    classes = target.shape[0]
    slots = blocks_here // shards
    chunk = max(slots, GROUP)
    chunks = classes * blocks_here // chunk
    half, rows, dests = chunk // 2, bl // parts, chunk // slots
    send_index, recv_index = routing(target, blocks_here, lax.axis_index("sec"), shards)
    smem, vmem = pl.BlockSpec(memory_space=pltpu.SMEM), pl.BlockSpec(memory_space=pltpu.VMEM)
    wide, narrow = jnp.float32, jnp.bfloat16
    flops = 4 * blocks_here * classes * left_ops.shape[1] * bl * bl * br
    return pl.pallas_call(
        functools.partial(kernel, (shards, classes, chunks, chunk, slots)),
        out_shape=jax.ShapeDtypeStruct((blocks_here, rows, br), wide),
        in_specs=[smem] * 4 + [vmem] * 3,
        out_specs=vmem,
        scratch_shapes=[
            pltpu.VMEM((chunks, chunk, parts, rows, br), wide),
            pltpu.VMEM((2, chunks, half, 2, rows, br), narrow),
            pltpu.VMEM((2, chunks, half, 2, rows, br), narrow),
            pltpu.VMEM((2, chunks, half, rows, br), narrow),
            pltpu.VMEM((2, chunks, half, rows, br), narrow),
            pltpu.VMEM((chunks, dests, slots, rows, br), narrow),
            pltpu.VMEM((classes, shards, slots, rows, br), narrow),
            pltpu.SemaphoreType.DMA((2, chunks)),
            pltpu.SemaphoreType.DMA((2, chunks)),
            pltpu.SemaphoreType.DMA((2, chunks)),
            pltpu.SemaphoreType.DMA((2, chunks)),
            pltpu.SemaphoreType.DMA((chunks, dests)),
            pltpu.SemaphoreType.DMA((classes, shards)),
        ],
        compiler_params=pltpu.CompilerParams(
            collective_id=0, has_side_effects=True, vmem_limit_bytes=48 * 1024 * 1024),
        cost_estimate=pl.CostEstimate(flops=flops, bytes_accessed=8 * 1024 * 1024, transcendentals=0),
    )(left_sector, right_sector, send_index, recv_index, wavefunction, left_ops, right_ops)


def solution(mesh):
    in_specs = (
        P("sec", None, None),
        P(None, "op", None, None, None),
        P(None, "op", None, None, None),
        P("sec"),
        P("sec"),
        P(),
    )
    out_specs = P("sec", "op", None)
    return jax.shard_map(
        per_device, mesh=mesh, in_specs=in_specs, out_specs=out_specs, check_vma=False
    )
```

time: 212 us -> 64.5 us (0.30)
  waiting for transfers between devices: 79.7 us -> 0 us
  matrix products: 59.7 us -> 0 us
  Pallas kernels: 0 us -> 56.6 us
  local copies, waits for them, and re-layouts: 43.7 us -> 6.21 us
  between operations: 13.6 us -> 0.04 us
  starting transfers between devices: 9.25 us -> 0 us
  other arithmetic: 5.14 us -> 1.37 us
    dot_general x8 -> x0, matrix products: 59.7 us -> none  [add_term(): jnp.einsum('bik,blk->bil', left_mixed, right_blocks, preferred_element_ty...]
    pallas_call x0 -> x1, Pallas kernels: none -> 56.6 us  [per_device(): pl.pallas_call(functools.partial(kernel, (shards, classes, chunks, chunk,...]
    reduce_scatter x2 -> x0, waiting for transfers between devices: 54.3 us -> none  [per_device(): share = lax.psum_scatter(summed, 'op', scatter_dimension=1, tiled=True)]
    gather x20 -> x0, local copies, waits for them, and re-layouts: 30 us -> none  [the longest x8 17.4 us: add_term(): left_blocks = jnp.take(left_term, left_sector, axis=0)]
    all_to_all x2 -> x0, waiting for transfers between devices: 25.3 us -> none  [per_device(): lax.all_to_all(jnp.take(share, send_index, axis=0), 'sec', split_axis=0,...]
    squeeze x11 -> x0, local copies, waits for them, and re-layouts: 13.1 us -> none  [the longest x8 8.53 us: class_terms(): running, _ = lax.scan(add_term, initial, (left_ops, right_ops))]
    all_to_all x2 -> x0, starting transfers between devices: 9.21 us -> none  [per_device(): lax.all_to_all(jnp.take(share, send_index, axis=0), 'sec', split_axis=0,...]
    unnamed x6 -> x9, local copies, waits for them, and re-layouts: 0.67 us -> 5.46 us
  transfers between devices with their start and end apart: 4 -> 0, of which waited for: 3 -> 0; matrix products, arithmetic and copies ran while one was open for 26% -> 0% of each run, Pallas kernels for 0% -> 0%
where the time goes in v1:
time: 64.5 us; the launch traced here: 64.3 us
  Pallas kernels  56.6 us (88%)
  local copies, waits for them, and re-layouts  6.21 us (10%)
  other arithmetic  1.37 us (2%)
    pallas_call x1, Pallas kernels, per_device(): pl.pallas_call(functools.partial(kernel, (shards, classes, chunks, chunk,...  56.6 us
    unnamed x9, local copies, waits for them, and re-layouts  5.46 us

profile of v1, /device:TPU:0, one launch (start us, length us, event | category | flops | bytes accessed | tf_op | source)
XLA Modules:
  0.0 64.3 jit_solution(1384279621880103145)
XLA Ops:
  0.0 0.7 %constant_dynamic-slice_fusion = s32[2,64]{1,0:T(2,128)S(1)} fusion(s32[2,512]{1,0:T(2,128)} %param.11, s32[]{:T(128)S(6)} %select_n.16), kind=kLoop, calls=%fused_computation.15 | loop fusion | bytes 1028 | tf_op jit(solution)/shard_map/dynamic_slice | solution.py:166
  0.8 0.2 convert_reduce_fusion.1
  0.9 0.1 select_reduce_fusion.1.send_sm
  1.1 0.9 %select_reduce_fusion = s32[2,64]{1,0:T(2,128)S(1)} fusion(s32[512]{0:T(512)S(1)} %add_select_fusion, s32[2,512]{1,0:T(2,128)} %param.11, s32[64]{0:T(128)S(1)} %iota_add_fusion), kind=kLoop, calls=%fused_computation | loop fusion | flops 196480 | bytes 6912 | tf_op jit(solution)/shard_map/reduce_sum | solution.py:171
  2.0 0.2 convert_reduce_fusion
  2.1 0.0 copy-start
  2.2 1.6 %copy-done = bf16[64,128,128]{2,1,0:T(8,128)(2,1)S(1)} copy-done((bf16[64,128,128]{2,1,0:T(8,128)(2,1)S(1)}, bf16[64,128,128]{2,1,0:T(8,128)(2,1)}, u32[]{:S(2)}) %copy-start) | copy-done | bytes 2097176
  3.7 0.0 copy-start.1
  3.7 1.6 %copy-done.1 = bf16[2,4,8,128,128]{4,3,2,1,0:T(8,128)(2,1)S(1)} copy-done((bf16[2,4,8,128,128]{4,3,2,1,0:T(8,128)(2,1)S(1)}, bf16[2,4,8,128,128]{4,3,2,1,0:T(8,128)(2,1)}, u32[]{:S(2)}) %copy-start.1) | copy-done | bytes 2097176
  5.3 0.0 copy-start.2
  5.3 0.7 %copy-done.2 = s32[64]{0:T(128)S(1)} copy-done((s32[64]{0:T(128)S(1)}, s32[64]{0:T(128)}, u32[]{:S(2)}) %copy-start.2) | copy-done | bytes 280
  6.0 0.0 copy-start.3
  6.0 0.7 %copy-done.3 = s32[64]{0:T(128)S(1)} copy-done((s32[64]{0:T(128)S(1)}, s32[64]{0:T(128)}, u32[]{:S(2)}) %copy-start.3) | copy-done | bytes 280
  6.6 56.6 %shard_map.64 = f32[64,32,128]{2,1,0:T(8,128)S(1)} custom-call(s32[64]{0:T(128)S(1)} %copy-done.2, s32[64]{0:T(128)S(1)} %copy-done.3, s32[2,64]{1,0:T(2,128)S(1)} %select_reduce_fusion.1.send_sm, s32[2,64]{1,0:T(2,128)S(1)} %multiply_add_fusion.recv_sm, bf16[64,128,128]{2,1,0:T(8,128)(2,1)S(1)} %copy-done, bf16[2,4,8,128,128]{4,3,2,1,0:T(8,128)(2,1)S(1)} %copy-done.1, ...), custom_call_target="tpu_custom_call" | custom-call | flops 4294967296 | bytes 8388608 | tf_op jit(solution)/shard_map/pallas_call | solution.py:190
  63.3 1.0 %copy.8 = f32[64,32,128]{2,1,0:T(8,128)} copy(f32[64,32,128]{2,1,0:T(8,128)S(1)} %shard_map.64) | data formatting | bytes 2097152
  (4 shorter events, 0.0 us)
Async XLA Ops:
  2.1 1.6 %copy-start = (bf16[64,128,128]{2,1,0:T(8,128)(2,1)S(1)}, bf16[64,128,128]{2,1,0:T(8,128)(2,1)}, u32[]{:S(2)}) copy-start(bf16[64,128,128]{2,1,0:T(8,128)(2,1)} %w_ref.1) | copy-start | bytes 6291460
  3.7 1.6 %copy-start.1 = (bf16[2,4,8,128,128]{4,3,2,1,0:T(8,128)(2,1)S(1)}, bf16[2,4,8,128,128]{4,3,2,1,0:T(8,128)(2,1)}, u32[]{:S(2)}) copy-start(bf16[2,4,8,128,128]{4,3,2,1,0:T(8,128)(2,1)} %l_ref.1) | copy-start | bytes 6291460
  5.3 0.7 %copy-start.2 = (s32[64]{0:T(128)S(1)}, s32[64]{0:T(128)}, u32[]{:S(2)}) copy-start(s32[64]{0:T(128)} %left_sm.1) | copy-start | bytes 772
  6.0 0.7 %copy-start.3 = (s32[64]{0:T(128)S(1)}, s32[64]{0:T(128)}, u32[]{:S(2)}) copy-start(s32[64]{0:T(128)} %right_sm.1) | copy-start | bytes 772

commit v2 on v1

--- a/solution.py
+++ b/solution.py
@@ -9,8 +9,8 @@
 
 MESH = pl.DeviceIdType.MESH
 GROUP = 8
-LAG_SECOND = 1
-LAG_ROUTE = 2
+LAG_SECOND = 2
+LAG_ROUTE = 4
 
 
 def kernel(sizes, left_sm, right_sm, send_sm, recv_sm, w_ref, l_ref, r_ref, out_ref,

time: 64.5 us -> 56.3 us (0.87)
  Pallas kernels: 56.6 us -> 48.4 us
    pallas_call x1, Pallas kernels: 56.6 us -> 48.4 us  [per_device(): pl.pallas_call(functools.partial(kernel, (shards, classes, chunks, chunk,...]
where the time goes in v2:
time: 56.3 us; the launch traced here: 56.1 us
  Pallas kernels  48.4 us (86%)
  local copies, waits for them, and re-layouts  6.21 us (11%)
  other arithmetic  1.37 us (2%)
    pallas_call x1, Pallas kernels, per_device(): pl.pallas_call(functools.partial(kernel, (shards, classes, chunks, chunk,...  48.4 us
    unnamed x9, local copies, waits for them, and re-layouts  5.46 us

profile of v2, /device:TPU:0, one launch (start us, length us, event | category | flops | bytes accessed | tf_op | source)
XLA Modules:
  0.0 56.1 jit_solution(13130474913021018195)
XLA Ops:
  0.0 0.7 %constant_dynamic-slice_fusion = s32[2,64]{1,0:T(2,128)S(1)} fusion(s32[2,512]{1,0:T(2,128)} %param.11, s32[]{:T(128)S(6)} %select_n.16), kind=kLoop, calls=%fused_computation.15 | loop fusion | bytes 1028 | tf_op jit(solution)/shard_map/dynamic_slice | solution.py:166
  0.8 0.2 convert_reduce_fusion.1
  0.9 0.1 select_reduce_fusion.1.send_sm
  1.1 0.9 %select_reduce_fusion = s32[2,64]{1,0:T(2,128)S(1)} fusion(s32[512]{0:T(512)S(1)} %add_select_fusion, s32[2,512]{1,0:T(2,128)} %param.11, s32[64]{0:T(128)S(1)} %iota_add_fusion), kind=kLoop, calls=%fused_computation | loop fusion | flops 196480 | bytes 6912 | tf_op jit(solution)/shard_map/reduce_sum | solution.py:171
  2.0 0.2 convert_reduce_fusion
  2.1 0.0 copy-start
  2.2 1.6 %copy-done = bf16[64,128,128]{2,1,0:T(8,128)(2,1)S(1)} copy-done((bf16[64,128,128]{2,1,0:T(8,128)(2,1)S(1)}, bf16[64,128,128]{2,1,0:T(8,128)(2,1)}, u32[]{:S(2)}) %copy-start) | copy-done | bytes 2097176
  3.7 0.0 copy-start.1
  3.7 1.6 %copy-done.1 = bf16[2,4,8,128,128]{4,3,2,1,0:T(8,128)(2,1)S(1)} copy-done((bf16[2,4,8,128,128]{4,3,2,1,0:T(8,128)(2,1)S(1)}, bf16[2,4,8,128,128]{4,3,2,1,0:T(8,128)(2,1)}, u32[]{:S(2)}) %copy-start.1) | copy-done | bytes 2097176
  5.3 0.0 copy-start.2
  5.3 0.7 %copy-done.2 = s32[64]{0:T(128)S(1)} copy-done((s32[64]{0:T(128)S(1)}, s32[64]{0:T(128)}, u32[]{:S(2)}) %copy-start.2) | copy-done | bytes 280
  6.0 0.0 copy-start.3
  6.0 0.7 %copy-done.3 = s32[64]{0:T(128)S(1)} copy-done((s32[64]{0:T(128)S(1)}, s32[64]{0:T(128)}, u32[]{:S(2)}) %copy-start.3) | copy-done | bytes 280
  6.6 48.4 %shard_map.64 = f32[64,32,128]{2,1,0:T(8,128)S(1)} custom-call(s32[64]{0:T(128)S(1)} %copy-done.2, s32[64]{0:T(128)S(1)} %copy-done.3, s32[2,64]{1,0:T(2,128)S(1)} %select_reduce_fusion.1.send_sm, s32[2,64]{1,0:T(2,128)S(1)} %multiply_add_fusion.recv_sm, bf16[64,128,128]{2,1,0:T(8,128)(2,1)S(1)} %copy-done, bf16[2,4,8,128,128]{4,3,2,1,0:T(8,128)(2,1)S(1)} %copy-done.1, ...), custom_call_target="tpu_custom_call" | custom-call | flops 4294967296 | bytes 8388608 | tf_op jit(solution)/shard_map/pallas_call | solution.py:190
  55.1 1.0 %copy.8 = f32[64,32,128]{2,1,0:T(8,128)} copy(f32[64,32,128]{2,1,0:T(8,128)S(1)} %shard_map.64) | data formatting | bytes 2097152
  (4 shorter events, 0.0 us)
Async XLA Ops:
  2.1 1.6 %copy-start = (bf16[64,128,128]{2,1,0:T(8,128)(2,1)S(1)}, bf16[64,128,128]{2,1,0:T(8,128)(2,1)}, u32[]{:S(2)}) copy-start(bf16[64,128,128]{2,1,0:T(8,128)(2,1)} %w_ref.1) | copy-start | bytes 6291460
  3.7 1.6 %copy-start.1 = (bf16[2,4,8,128,128]{4,3,2,1,0:T(8,128)(2,1)S(1)}, bf16[2,4,8,128,128]{4,3,2,1,0:T(8,128)(2,1)}, u32[]{:S(2)}) copy-start(bf16[2,4,8,128,128]{4,3,2,1,0:T(8,128)(2,1)} %l_ref.1) | copy-start | bytes 6291460
  5.3 0.7 %copy-start.2 = (s32[64]{0:T(128)S(1)}, s32[64]{0:T(128)}, u32[]{:S(2)}) copy-start(s32[64]{0:T(128)} %left_sm.1) | copy-start | bytes 772
  6.0 0.7 %copy-start.3 = (s32[64]{0:T(128)S(1)}, s32[64]{0:T(128)}, u32[]{:S(2)}) copy-start(s32[64]{0:T(128)} %right_sm.1) | copy-start | bytes 772

commit v3 on v2

--- a/solution.py
+++ b/solution.py
@@ -13,11 +13,38 @@
 LAG_ROUTE = 4
 
 
-def kernel(sizes, left_sm, right_sm, send_sm, recv_sm, w_ref, l_ref, r_ref, out_ref,
-           acc, s1, r1, s2, r2, s3, arr, sem_s1, sem_r1, sem_s2, sem_r2, sem_s3, sem_r3):
+def fill_tables(target_ref, table, me, shards, slots):
+    classes, total = target_ref.shape
+    n = total // shards
+    block = lax.broadcasted_iota(jnp.int32, (n, total), 1)
+    here = me * n + lax.broadcasted_iota(jnp.int32, (n, total), 0)
+    row, col = (lax.broadcasted_iota(jnp.int32, (n, n), axis) for axis in range(2))
+    bound = (lax.broadcasted_iota(jnp.int32, (n, shards), 1) + 1) * n
+
+    def count(mask):
+        return jnp.sum(jnp.where(mask, 1, 0), axis=1, keepdims=True)
+
+    def as_row(column):
+        return jnp.sum(jnp.where(row == col, column, 0), axis=0, keepdims=True)
+
+    for q in range(classes):
+        target = target_ref[q:q + 1, :]
+        mine = jnp.sum(jnp.where(block == here, target, 0), axis=1, keepdims=True)
+        position = count(as_row(mine) < mine)
+        order = jnp.sum(jnp.where(position == col, row, 0), axis=0, keepdims=True)
+        table[q:q + 1, 0:n] = jnp.minimum(order, n - 1)
+        origin = jnp.sum(jnp.where(target == here, block, 0), axis=1, keepdims=True)
+        source = count(origin >= bound)
+        rank = count((as_row(source) == source) & (col < row))
+        table[classes + q:classes + q + 1, 0:n] = jnp.minimum(as_row(source * slots + rank), n - 1)
+
+
+def kernel(sizes, left_sm, right_sm, target_ref, w_any, l_any, r_any, out_ref,
+           w_ref, l_refs, r_refs, table, table_sm, acc, s1, r1, s2, r2, s3, arr,
+           sem_in, sem_s1, sem_r1, sem_s2, sem_r2, sem_s3, sem_r3):
     shards, classes, chunks, chunk, slots = sizes
     half = chunk // 2
-    terms, bl = l_ref.shape[1], l_ref.shape[3]
+    terms, bl = l_any.shape[1], l_any.shape[3]
     rows = acc.shape[3]
     op, me = lax.axis_index("op"), lax.axis_index("sec")
     hi, lo = op // 2, op % 2
@@ -29,6 +56,16 @@
         off = shards // 2 + (1 - 2 * (k % 2)) * ((k + 1) // 2)
         return (me + off + shards) % shards
 
+    pieces = classes * terms
+    part = w_ref.shape[0] // pieces
+    for u in range(pieces):
+        span = pl.ds(u * part, part)
+        pltpu.make_async_copy(w_any.at[span], w_ref.at[span], sem_in.at[2 * classes]).start()
+    for q in range(classes):
+        for t in range(terms):
+            pltpu.make_async_copy(l_any.at[q, t], l_refs[q].at[t], sem_in.at[q]).start()
+            pltpu.make_async_copy(r_any.at[q, t], r_refs[q].at[t], sem_in.at[classes + q]).start()
+
     barrier = pltpu.get_barrier_semaphore()
     for other in (near_lo, near_hi):
         pl.semaphore_signal(barrier, inc=1, device_id={"op": other}, device_id_type=MESH)
@@ -38,6 +75,11 @@
         return carry
 
     lax.fori_loop(0, shards - 1, greet, 0)
+    fill_tables(target_ref, table, me, shards, slots)
+    copy = pltpu.make_async_copy(table, table_sm, sem_in.at[2 * classes + 1])
+    copy.start()
+    copy.wait()
+    pltpu.make_async_copy(w_any, w_ref, sem_in.at[2 * classes]).wait()
     pl.semaphore_wait(barrier, 2 + shards - 1)
 
     def first_copy(h, i):
@@ -55,20 +97,28 @@
             src_ref=s3.at[i, e], dst_ref=arr.at[q, me], send_sem=sem_s3.at[i, e], recv_sem=sem_r3.at[q, me],
             device_id={"sec": peer(k)}, device_id_type=MESH)
 
-    def compute(i):
-        q, c = i % classes, i // classes
+    def compute(i, q):
+        c = i // classes
+
+        @pl.when(i < classes)
+        def _():
+            pltpu.make_async_copy(l_any.at[q], l_refs[q], sem_in.at[q]).wait()
+            pltpu.make_async_copy(r_any.at[q], r_refs[q], sem_in.at[classes + q]).wait()
+
         for b in range(chunk):
             dest = peer(c * dests + b // slots)
-            block = send_sm[q, dest * slots + b % slots]
+            block = table_sm[q, dest * slots + b % slots]
             left = left_sm[block]
             right = right_sm[block]
             mixed = jnp.dot(
-                l_ref[q, :, left].reshape(terms * bl, l_ref.shape[4]), w_ref[block],
+                l_refs[q][:, left].reshape(terms * bl, l_any.shape[4]), w_ref[block],
                 preferred_element_type=jnp.float32).astype(jnp.bfloat16)
             mixed = jnp.concatenate([mixed[t * bl:(t + 1) * bl] for t in range(terms)], axis=1)
-            rights = jnp.concatenate([r_ref[q, t, right] for t in range(terms)], axis=1)
+            rights = jnp.concatenate([r_refs[q][t, right] for t in range(terms)], axis=1)
             value = lax.dot_general(mixed, rights, (((1,), (1,)), ((), ())), preferred_element_type=jnp.float32)
             acc[i, b] = value.reshape(acc.shape[2:])
+
+    def first(i):
         for j in range(2):
             s1[0, i, :, j] = acc[i, 0:half, j * 2 + 1 - lo].astype(jnp.bfloat16)
         first_copy(0, i).start()
@@ -108,7 +158,9 @@
     def step(i, carry):
         @pl.when(i < chunks)
         def _():
-            compute(i)
+            for q in range(classes):
+                pl.when(i % classes == q)(functools.partial(compute, i, q))
+            first(i)
 
         @pl.when((i >= LAG_SECOND) & (i < chunks + LAG_SECOND))
         def _():
@@ -137,7 +189,7 @@
             slot = n * GROUP + u
             total = None
             for q in range(classes):
-                at = recv_sm[q, slot]
+                at = table_sm[classes + q, slot]
                 here = arr[q, at // slots, at % slots].astype(jnp.float32)
                 total = here if total is None else total + here
             out_ref[slot] = total
@@ -158,20 +210,6 @@
         return carry
 
     lax.fori_loop(0, chunks, drain, 0)
-
-
-def routing(target, blocks_here, own_index, shards):
-    slots = blocks_here // shards
-    slot_ids = jnp.arange(blocks_here, dtype=jnp.int32)
-    mine = lax.dynamic_slice_in_dim(target, own_index * blocks_here, blocks_here, 1)
-    position = jnp.sum((mine[:, None, :] < mine[:, :, None]).astype(jnp.int32), axis=2)
-    send_index = jnp.sum(jnp.where(position[:, None, :] == slot_ids[:, None], slot_ids, 0), axis=2)
-    wanted = own_index * blocks_here + slot_ids
-    devices = jnp.arange(target.shape[1], dtype=jnp.int32) // blocks_here
-    source = jnp.sum(jnp.where(target[:, None, :] == wanted[:, None], devices, 0), axis=2)
-    same = (source[:, None, :] == source[:, :, None]) & (slot_ids[None, :] < slot_ids[:, None])
-    recv_index = source * slots + jnp.sum(same.astype(jnp.int32), axis=2)
-    return send_index, recv_index
 
 
 def per_device(wavefunction, left_ops, right_ops, left_sector, right_sector, target):
@@ -183,16 +221,21 @@
     chunk = max(slots, GROUP)
     chunks = classes * blocks_here // chunk
     half, rows, dests = chunk // 2, bl // parts, chunk // slots
-    send_index, recv_index = routing(target, blocks_here, lax.axis_index("sec"), shards)
+    table = (2 * classes + -2 * classes % 8, blocks_here + -blocks_here % 128)
     smem, vmem = pl.BlockSpec(memory_space=pltpu.SMEM), pl.BlockSpec(memory_space=pltpu.VMEM)
     wide, narrow = jnp.float32, jnp.bfloat16
     flops = 4 * blocks_here * classes * left_ops.shape[1] * bl * bl * br
     return pl.pallas_call(
         functools.partial(kernel, (shards, classes, chunks, chunk, slots)),
         out_shape=jax.ShapeDtypeStruct((blocks_here, rows, br), wide),
-        in_specs=[smem] * 4 + [vmem] * 3,
+        in_specs=[smem] * 2 + [vmem] + [pl.BlockSpec(memory_space=pl.ANY)] * 3,
         out_specs=vmem,
         scratch_shapes=[
+            pltpu.VMEM(wavefunction.shape, wavefunction.dtype),
+            [pltpu.VMEM(left_ops.shape[1:], left_ops.dtype)] * classes,
+            [pltpu.VMEM(right_ops.shape[1:], right_ops.dtype)] * classes,
+            pltpu.VMEM(table, jnp.int32),
+            pltpu.SMEM(table, jnp.int32),
             pltpu.VMEM((chunks, chunk, parts, rows, br), wide),
             pltpu.VMEM((2, chunks, half, 2, rows, br), narrow),
             pltpu.VMEM((2, chunks, half, 2, rows, br), narrow),
@@ -200,6 +243,7 @@
             pltpu.VMEM((2, chunks, half, rows, br), narrow),
             pltpu.VMEM((chunks, dests, slots, rows, br), narrow),
             pltpu.VMEM((classes, shards, slots, rows, br), narrow),
+            pltpu.SemaphoreType.DMA((2 * classes + 2,)),
             pltpu.SemaphoreType.DMA((2, chunks)),
             pltpu.SemaphoreType.DMA((2, chunks)),
             pltpu.SemaphoreType.DMA((2, chunks)),
@@ -208,9 +252,9 @@
             pltpu.SemaphoreType.DMA((classes, shards)),
         ],
         compiler_params=pltpu.CompilerParams(
-            collective_id=0, has_side_effects=True, vmem_limit_bytes=48 * 1024 * 1024),
+            collective_id=0, has_side_effects=True, vmem_limit_bytes=56 * 1024 * 1024),
         cost_estimate=pl.CostEstimate(flops=flops, bytes_accessed=8 * 1024 * 1024, transcendentals=0),
-    )(left_sector, right_sector, send_index, recv_index, wavefunction, left_ops, right_ops)
+    )(left_sector, right_sector, target, wavefunction, left_ops, right_ops)
 
 
 def solution(mesh):

time: 56.3 us -> 51.1 us (0.908)
  local copies, waits for them, and re-layouts: 6.21 us -> 2.26 us
  other arithmetic: 1.37 us -> 0 us
    unnamed x9 -> x1, local copies, waits for them, and re-layouts: 5.46 us -> 2.26 us
    reduce_sum x4 -> x0, other arithmetic: 1.35 us -> none  [the longest x1 0.88 us: routing(): jnp.sum(jnp.where(target[:, None, :] == wanted[:, None], devices, 0), axi...]
    dynamic_slice x1 -> x0, local copies, waits for them, and re-layouts: 0.75 us -> none  [routing(): lax.dynamic_slice_in_dim(target, own_index * blocks_here, blocks_here, 1)]
where the time goes in v3:
time: 51.1 us; the launch traced here: 50.9 us
  Pallas kernels  48.6 us (95%)
  local copies, waits for them, and re-layouts  2.26 us (4%)
    pallas_call x1, Pallas kernels, per_device(): pl.pallas_call(functools.partial(kernel, (shards, classes, chunks, chunk,...  48.6 us
    unnamed x1, local copies, waits for them, and re-layouts  2.26 us

profile of v3, /device:TPU:0, one launch (start us, length us, event | category | flops | bytes accessed | tf_op | source)
XLA Modules:
  0.0 50.9 jit_solution(1044243396759415115)
XLA Ops:
  0.0 48.6 %shard_map.64 = f32[64,32,128]{2,1,0:T(8,128)} custom-call(s32[64]{0:T(128)} %left_sm.1, s32[64]{0:T(128)} %right_sm.1, s32[2,512]{1,0:T(2,128)} %target_ref.1, bf16[64,128,128]{2,1,0:T(8,128)(2,1)} %w_any.1, bf16[2,4,8,128,128]{4,3,2,1,0:T(8,128)(2,1)} %l_any.1, bf16[2,4,8,128,128]{4,3,2,1,0:T(8,128)(2,1)} %r_any.1), custom_call_target="tpu_custom_call" | custom-call | flops 4294967296 | bytes 8388608 | tf_op jit(solution)/shard_map/pallas_call | solution.py:228
  48.6 2.3 %copy.8 = f32[64,32,128]{2,1,0:T(8,128)} copy(f32[64,32,128]{2,1,0:T(8,128)} %shard_map.64) | data formatting | bytes 2097152

commit v4 on v3

--- a/solution.py
+++ b/solution.py
@@ -8,9 +8,9 @@
 from jax.sharding import PartitionSpec as P
 
 MESH = pl.DeviceIdType.MESH
-GROUP = 8
-LAG_SECOND = 2
-LAG_ROUTE = 4
+GROUP = 4
+LAG_SECOND = 4
+LAG_ROUTE = 8
 
 
 def fill_tables(target_ref, table, me, shards, slots):
@@ -50,7 +50,7 @@
     hi, lo = op // 2, op % 2
     own = hi * 2 + lo
     near_lo, near_hi = hi * 2 + 1 - lo, (1 - hi) * 2 + lo
-    dests = chunk // slots
+    run = min(chunk, slots)
 
     def peer(k):
         off = shards // 2 + (1 - 2 * (k % 2)) * ((k + 1) // 2)
@@ -92,9 +92,10 @@
             src_ref=s2.at[h, i], dst_ref=r2.at[h, i], send_sem=sem_s2.at[h, i], recv_sem=sem_r2.at[h, i],
             device_id={"op": near_hi if h == 0 else near_lo}, device_id_type=MESH)
 
-    def route_copy(i, e, q, k):
+    def route_copy(i, e, q, k, part):
         return pltpu.make_async_remote_copy(
-            src_ref=s3.at[i, e], dst_ref=arr.at[q, me], send_sem=sem_s3.at[i, e], recv_sem=sem_r3.at[q, me],
+            src_ref=s3.at[i, e], dst_ref=arr.at[q, me, part], send_sem=sem_s3.at[i, e],
+            recv_sem=sem_r3.at[q, me, part],
             device_id={"sec": peer(k)}, device_id_type=MESH)
 
     def compute(i, q):
@@ -106,8 +107,8 @@
             pltpu.make_async_copy(r_any.at[q], r_refs[q], sem_in.at[classes + q]).wait()
 
         for b in range(chunk):
-            dest = peer(c * dests + b // slots)
-            block = table_sm[q, dest * slots + b % slots]
+            place_at = c * chunk + b
+            block = table_sm[q, peer(place_at // slots) * slots + place_at % slots]
             left = left_sm[block]
             right = right_sm[block]
             mixed = jnp.dot(
@@ -142,18 +143,19 @@
             second_copy(h, i).wait_recv()
             total = acc[i, h * half:(h + 1) * half, own] + r2[h, i].astype(jnp.float32)
             acc[i, h * half:(h + 1) * half, own] = total
-        for e in range(dests):
-            k = c * dests + e
-            share = acc[i, e * slots:(e + 1) * slots, own].astype(jnp.bfloat16)
+        for e in range(chunk // run):
+            at = c * chunk + e * run
+            k, part = at // slots, (at % slots) // run
+            share = acc[i, e * run:(e + 1) * run, own].astype(jnp.bfloat16)
 
             @pl.when(k < shards - 1)
             def _():
                 s3[i, e] = share
-                route_copy(i, e, q, k).start()
+                route_copy(i, e, q, k, part).start()
 
             @pl.when(k == shards - 1)
             def _():
-                arr[q, me] = share
+                arr[q, me, part] = share
 
     def step(i, carry):
         @pl.when(i < chunks)
@@ -177,9 +179,11 @@
     def arrive(k, carry):
         source = peer(k)
         for q in range(classes):
-            pltpu.make_async_remote_copy(
-                src_ref=s3.at[0, 0], dst_ref=arr.at[q, source], send_sem=sem_s3.at[0, 0],
-                recv_sem=sem_r3.at[q, source], device_id={"sec": source}, device_id_type=MESH).wait_recv()
+            for part in range(slots // run):
+                pltpu.make_async_remote_copy(
+                    src_ref=s3.at[0, 0], dst_ref=arr.at[q, source, part], send_sem=sem_s3.at[0, 0],
+                    recv_sem=sem_r3.at[q, source, part], device_id={"sec": source},
+                    device_id_type=MESH).wait_recv()
         return carry
 
     lax.fori_loop(0, shards - 1, arrive, 0)
@@ -190,7 +194,7 @@
             total = None
             for q in range(classes):
                 at = table_sm[classes + q, slot]
-                here = arr[q, at // slots, at % slots].astype(jnp.float32)
+                here = arr[q, at // slots, (at % slots) // run, at % run].astype(jnp.float32)
                 total = here if total is None else total + here
             out_ref[slot] = total
         return carry
@@ -201,12 +205,13 @@
         for h in range(2):
             first_copy(h, i).wait_send()
             second_copy(h, i).wait_send()
-        for e in range(dests):
-            k = (i // classes) * dests + e
+        for e in range(chunk // run):
+            at = (i // classes) * chunk + e * run
+            k, part = at // slots, (at % slots) // run
 
             @pl.when(k < shards - 1)
             def _():
-                route_copy(i, e, i % classes, k).wait_send()
+                route_copy(i, e, i % classes, k, part).wait_send()
         return carry
 
     lax.fori_loop(0, chunks, drain, 0)
@@ -218,9 +223,10 @@
     blocks_here, bl, br = wavefunction.shape
     classes = target.shape[0]
     slots = blocks_here // shards
-    chunk = max(slots, GROUP)
+    chunk = min(blocks_here, GROUP)
     chunks = classes * blocks_here // chunk
-    half, rows, dests = chunk // 2, bl // parts, chunk // slots
+    run = min(chunk, slots)
+    half, rows, dests = chunk // 2, bl // parts, chunk // run
     table = (2 * classes + -2 * classes % 8, blocks_here + -blocks_here % 128)
     smem, vmem = pl.BlockSpec(memory_space=pltpu.SMEM), pl.BlockSpec(memory_space=pltpu.VMEM)
     wide, narrow = jnp.float32, jnp.bfloat16
@@ -241,15 +247,15 @@
             pltpu.VMEM((2, chunks, half, 2, rows, br), narrow),
             pltpu.VMEM((2, chunks, half, rows, br), narrow),
             pltpu.VMEM((2, chunks, half, rows, br), narrow),
-            pltpu.VMEM((chunks, dests, slots, rows, br), narrow),
-            pltpu.VMEM((classes, shards, slots, rows, br), narrow),
+            pltpu.VMEM((chunks, dests, run, rows, br), narrow),
+            pltpu.VMEM((classes, shards, slots // run, run, rows, br), narrow),
             pltpu.SemaphoreType.DMA((2 * classes + 2,)),
             pltpu.SemaphoreType.DMA((2, chunks)),
             pltpu.SemaphoreType.DMA((2, chunks)),
             pltpu.SemaphoreType.DMA((2, chunks)),
             pltpu.SemaphoreType.DMA((2, chunks)),
             pltpu.SemaphoreType.DMA((chunks, dests)),
-            pltpu.SemaphoreType.DMA((classes, shards)),
+            pltpu.SemaphoreType.DMA((classes, shards, slots // run)),
         ],
         compiler_params=pltpu.CompilerParams(
             collective_id=0, has_side_effects=True, vmem_limit_bytes=56 * 1024 * 1024),

time: 51.1 us -> 53.9 us (1.055)
  Pallas kernels: 48.6 us -> 51.4 us
    pallas_call x1, Pallas kernels: 48.6 us -> 51.4 us  [per_device(): pl.pallas_call(functools.partial(kernel, (shards, classes, chunks, chunk,...]
where the time goes in v4:
time: 53.9 us; the launch traced here: 53.7 us
  Pallas kernels  51.4 us (95%)
  local copies, waits for them, and re-layouts  2.26 us (4%)
    pallas_call x1, Pallas kernels, per_device(): pl.pallas_call(functools.partial(kernel, (shards, classes, chunks, chunk,...  51.4 us
    unnamed x1, local copies, waits for them, and re-layouts  2.26 us

profile of v4, /device:TPU:0, one launch (start us, length us, event | category | flops | bytes accessed | tf_op | source)
XLA Modules:
  0.0 53.7 jit_solution(13884293041566009803)
XLA Ops:
  0.0 51.4 %shard_map.64 = f32[64,32,128]{2,1,0:T(8,128)} custom-call(s32[64]{0:T(128)} %left_sm.1, s32[64]{0:T(128)} %right_sm.1, s32[2,512]{1,0:T(2,128)} %target_ref.1, bf16[64,128,128]{2,1,0:T(8,128)(2,1)} %w_any.1, bf16[2,4,8,128,128]{4,3,2,1,0:T(8,128)(2,1)} %l_any.1, bf16[2,4,8,128,128]{4,3,2,1,0:T(8,128)(2,1)} %r_any.1), custom_call_target="tpu_custom_call" | custom-call | flops 4294967296 | bytes 8388608 | tf_op jit(solution)/shard_map/pallas_call | solution.py:234
  51.4 2.3 %copy.8 = f32[64,32,128]{2,1,0:T(8,128)} copy(f32[64,32,128]{2,1,0:T(8,128)} %shard_map.64) | data formatting | bytes 2097152

commit v5 on v4

--- a/solution.py
+++ b/solution.py
@@ -8,9 +8,9 @@
 from jax.sharding import PartitionSpec as P
 
 MESH = pl.DeviceIdType.MESH
-GROUP = 4
-LAG_SECOND = 4
-LAG_ROUTE = 8
+GROUP = 8
+LAG_SECOND = 2
+LAG_ROUTE = 4
 
 
 def fill_tables(target_ref, table, me, shards, slots):
@@ -106,6 +106,13 @@
             pltpu.make_async_copy(l_any.at[q], l_refs[q], sem_in.at[q]).wait()
             pltpu.make_async_copy(r_any.at[q], r_refs[q], sem_in.at[classes + q]).wait()
 
+            def turn(sector, carry):
+                for t in range(terms):
+                    r_refs[q][t, sector] = r_refs[q][t, sector].T
+                return carry
+
+            lax.fori_loop(0, r_any.shape[2], turn, 0)
+
         for b in range(chunk):
             place_at = c * chunk + b
             block = table_sm[q, peer(place_at // slots) * slots + place_at % slots]
@@ -115,8 +122,8 @@
                 l_refs[q][:, left].reshape(terms * bl, l_any.shape[4]), w_ref[block],
                 preferred_element_type=jnp.float32).astype(jnp.bfloat16)
             mixed = jnp.concatenate([mixed[t * bl:(t + 1) * bl] for t in range(terms)], axis=1)
-            rights = jnp.concatenate([r_refs[q][t, right] for t in range(terms)], axis=1)
-            value = lax.dot_general(mixed, rights, (((1,), (1,)), ((), ())), preferred_element_type=jnp.float32)
+            rights = r_refs[q][:, right].reshape(terms * r_any.shape[4], r_any.shape[3])
+            value = jnp.dot(mixed, rights, preferred_element_type=jnp.float32)
             acc[i, b] = value.reshape(acc.shape[2:])
 
     def first(i):

time: 53.9 us -> 52.7 us (0.978)
  Pallas kernels: 51.4 us -> 50.3 us
    pallas_call x1, Pallas kernels: 51.4 us -> 50.3 us  [per_device(): pl.pallas_call(functools.partial(kernel, (shards, classes, chunks, chunk,...]
where the time goes in v5:
time: 52.7 us; the launch traced here: 52.5 us
  Pallas kernels  50.3 us (95%)
  local copies, waits for them, and re-layouts  2.26 us (4%)
    pallas_call x1, Pallas kernels, per_device(): pl.pallas_call(functools.partial(kernel, (shards, classes, chunks, chunk,...  50.3 us
    unnamed x1, local copies, waits for them, and re-layouts  2.26 us

profile of v5, /device:TPU:0, one launch (start us, length us, event | category | flops | bytes accessed | tf_op | source)
XLA Modules:
  0.0 52.5 jit_solution(13100364850416423374)
XLA Ops:
  0.0 50.3 %shard_map.64 = f32[64,32,128]{2,1,0:T(8,128)} custom-call(s32[64]{0:T(128)} %left_sm.1, s32[64]{0:T(128)} %right_sm.1, s32[2,512]{1,0:T(2,128)} %target_ref.1, bf16[64,128,128]{2,1,0:T(8,128)(2,1)} %w_any.1, bf16[2,4,8,128,128]{4,3,2,1,0:T(8,128)(2,1)} %l_any.1, bf16[2,4,8,128,128]{4,3,2,1,0:T(8,128)(2,1)} %r_any.1), custom_call_target="tpu_custom_call" | custom-call | flops 4294967296 | bytes 8388608 | tf_op jit(solution)/shard_map/pallas_call | solution.py:241
  50.3 2.3 %copy.8 = f32[64,32,128]{2,1,0:T(8,128)} copy(f32[64,32,128]{2,1,0:T(8,128)} %shard_map.64) | data formatting | bytes 2097152

commit v6 on v4

--- a/solution.py
+++ b/solution.py
@@ -8,9 +8,9 @@
 from jax.sharding import PartitionSpec as P
 
 MESH = pl.DeviceIdType.MESH
-GROUP = 4
-LAG_SECOND = 4
-LAG_ROUTE = 8
+GROUP = 8
+LAG_SECOND = 3
+LAG_ROUTE = 6
 
 
 def fill_tables(target_ref, table, me, shards, slots):
@@ -80,8 +80,6 @@
     copy.start()
     copy.wait()
     pltpu.make_async_copy(w_any, w_ref, sem_in.at[2 * classes]).wait()
-    pl.semaphore_wait(barrier, 2 + shards - 1)
-
     def first_copy(h, i):
         return pltpu.make_async_remote_copy(
             src_ref=s1.at[h, i], dst_ref=r1.at[h, i], send_sem=sem_s1.at[h, i], recv_sem=sem_r1.at[h, i],
@@ -101,7 +99,7 @@
     def compute(i, q):
         c = i // classes
 
-        @pl.when(i < classes)
+        @pl.when(jnp.int32(i) < classes)
         def _():
             pltpu.make_async_copy(l_any.at[q], l_refs[q], sem_in.at[q]).wait()
             pltpu.make_async_copy(r_any.at[q], r_refs[q], sem_in.at[classes + q]).wait()
@@ -161,7 +159,7 @@
         @pl.when(i < chunks)
         def _():
             for q in range(classes):
-                pl.when(i % classes == q)(functools.partial(compute, i, q))
+                pl.when((i % classes == q) & (i > 0))(functools.partial(compute, i, q))
             first(i)
 
         @pl.when((i >= LAG_SECOND) & (i < chunks + LAG_SECOND))
@@ -174,6 +172,8 @@
 
         return carry
 
+    compute(0, 0)
+    pl.semaphore_wait(barrier, 2 + shards - 1)
     lax.fori_loop(0, chunks + LAG_ROUTE, step, 0)
 
     def arrive(k, carry):

time: 53.9 us -> 50.5 us (0.937)
  Pallas kernels: 51.4 us -> 47.8 us
    pallas_call x1, Pallas kernels: 51.4 us -> 47.8 us  [per_device(): pl.pallas_call(functools.partial(kernel, (shards, classes, chunks, chunk,...]
where the time goes in v6:
time: 50.5 us; the launch traced here: 50.1 us
  Pallas kernels  47.8 us (95%)
  local copies, waits for them, and re-layouts  2.26 us (4%)
    pallas_call x1, Pallas kernels, per_device(): pl.pallas_call(functools.partial(kernel, (shards, classes, chunks, chunk,...  47.8 us
    unnamed x1, local copies, waits for them, and re-layouts  2.26 us

profile of v6, /device:TPU:0, one launch (start us, length us, event | category | flops | bytes accessed | tf_op | source)
XLA Modules:
  0.0 50.1 jit_solution(7849041641334007026)
XLA Ops:
  0.0 47.8 %shard_map.64 = f32[64,32,128]{2,1,0:T(8,128)} custom-call(s32[64]{0:T(128)} %left_sm.1, s32[64]{0:T(128)} %right_sm.1, s32[2,512]{1,0:T(2,128)} %target_ref.1, bf16[64,128,128]{2,1,0:T(8,128)(2,1)} %w_any.1, bf16[2,4,8,128,128]{4,3,2,1,0:T(8,128)(2,1)} %l_any.1, bf16[2,4,8,128,128]{4,3,2,1,0:T(8,128)(2,1)} %r_any.1), custom_call_target="tpu_custom_call" | custom-call | flops 4294967296 | bytes 8388608 | tf_op jit(solution)/shard_map/pallas_call | solution.py:234
  47.8 2.3 %copy.8 = f32[64,32,128]{2,1,0:T(8,128)} copy(f32[64,32,128]{2,1,0:T(8,128)} %shard_map.64) | data formatting | bytes 2097152

commit v7 on v6

--- a/solution.py
+++ b/solution.py
@@ -9,6 +9,7 @@
 
 MESH = pl.DeviceIdType.MESH
 GROUP = 8
+BESIDE = 4
 LAG_SECOND = 3
 LAG_ROUTE = 6
 
@@ -104,18 +105,25 @@
             pltpu.make_async_copy(l_any.at[q], l_refs[q], sem_in.at[q]).wait()
             pltpu.make_async_copy(r_any.at[q], r_refs[q], sem_in.at[classes + q]).wait()
 
-        for b in range(chunk):
-            place_at = c * chunk + b
-            block = table_sm[q, peer(place_at // slots) * slots + place_at % slots]
-            left = left_sm[block]
-            right = right_sm[block]
-            mixed = jnp.dot(
-                l_refs[q][:, left].reshape(terms * bl, l_any.shape[4]), w_ref[block],
-                preferred_element_type=jnp.float32).astype(jnp.bfloat16)
-            mixed = jnp.concatenate([mixed[t * bl:(t + 1) * bl] for t in range(terms)], axis=1)
-            rights = jnp.concatenate([r_refs[q][t, right] for t in range(terms)], axis=1)
-            value = lax.dot_general(mixed, rights, (((1,), (1,)), ((), ())), preferred_element_type=jnp.float32)
-            acc[i, b] = value.reshape(acc.shape[2:])
+        for start in range(0, chunk, BESIDE):
+            spots = []
+            for b in range(start, min(start + BESIDE, chunk)):
+                place_at = c * chunk + b
+                block = table_sm[q, peer(place_at // slots) * slots + place_at % slots]
+                spots.append((b, block, left_sm[block], right_sm[block]))
+            mixes = []
+            for b, block, left, right in spots:
+                mixed = jnp.dot(
+                    l_refs[q][:, left].reshape(terms * bl, l_any.shape[4]), w_ref[block],
+                    preferred_element_type=jnp.float32).astype(jnp.bfloat16)
+                mixes.append(jnp.concatenate([mixed[t * bl:(t + 1) * bl] for t in range(terms)], axis=1))
+            values = []
+            for (b, block, left, right), mixed in zip(spots, mixes):
+                rights = jnp.concatenate([r_refs[q][t, right] for t in range(terms)], axis=1)
+                values.append(lax.dot_general(
+                    mixed, rights, (((1,), (1,)), ((), ())), preferred_element_type=jnp.float32))
+            for (b, block, left, right), value in zip(spots, values):
+                acc[i, b] = value.reshape(acc.shape[2:])
 
     def first(i):
         for j in range(2):

time: 50.5 us -> 50.4 us (level)
  no operation moved by 1% of the time
where the time goes in v7:
time: 50.4 us; the launch traced here: 50.1 us
  Pallas kernels  47.9 us (95%)
  local copies, waits for them, and re-layouts  2.26 us (4%)
    pallas_call x1, Pallas kernels, per_device(): pl.pallas_call(functools.partial(kernel, (shards, classes, chunks, chunk,...  47.9 us
    unnamed x1, local copies, waits for them, and re-layouts  2.26 us

profile of v7, /device:TPU:0, one launch (start us, length us, event | category | flops | bytes accessed | tf_op | source)
XLA Modules:
  0.0 50.1 jit_solution(4934450484820622291)
XLA Ops:
  0.0 47.9 %shard_map.64 = f32[64,32,128]{2,1,0:T(8,128)} custom-call(s32[64]{0:T(128)} %left_sm.1, s32[64]{0:T(128)} %right_sm.1, s32[2,512]{1,0:T(2,128)} %target_ref.1, bf16[64,128,128]{2,1,0:T(8,128)(2,1)} %w_any.1, bf16[2,4,8,128,128]{4,3,2,1,0:T(8,128)(2,1)} %l_any.1, bf16[2,4,8,128,128]{4,3,2,1,0:T(8,128)(2,1)} %r_any.1), custom_call_target="tpu_custom_call" | custom-call | flops 4294967296 | bytes 8388608 | tf_op jit(solution)/shard_map/pallas_call | solution.py:242
  47.9 2.3 %copy.8 = f32[64,32,128]{2,1,0:T(8,128)} copy(f32[64,32,128]{2,1,0:T(8,128)} %shard_map.64) | data formatting | bytes 2097152

commit v8 on v7

--- a/solution.py
+++ b/solution.py
@@ -14,9 +14,10 @@
 LAG_ROUTE = 6
 
 
-def fill_tables(target_ref, table, me, shards, slots):
-    classes, total = target_ref.shape
+def fill_tables(whole_ref, classes, table, me, shards, slots):
+    total = whole_ref.shape[1]
     n = total // shards
+    table[2 * classes:2 * classes + 2, 0:n] = whole_ref[classes:classes + 2, 0:n]
     block = lax.broadcasted_iota(jnp.int32, (n, total), 1)
     here = me * n + lax.broadcasted_iota(jnp.int32, (n, total), 0)
     row, col = (lax.broadcasted_iota(jnp.int32, (n, n), axis) for axis in range(2))
@@ -29,7 +30,7 @@
         return jnp.sum(jnp.where(row == col, column, 0), axis=0, keepdims=True)
 
     for q in range(classes):
-        target = target_ref[q:q + 1, :]
+        target = whole_ref[q:q + 1, :]
         mine = jnp.sum(jnp.where(block == here, target, 0), axis=1, keepdims=True)
         position = count(as_row(mine) < mine)
         order = jnp.sum(jnp.where(position == col, row, 0), axis=0, keepdims=True)
@@ -40,7 +41,7 @@
         table[classes + q:classes + q + 1, 0:n] = jnp.minimum(as_row(source * slots + rank), n - 1)
 
 
-def kernel(sizes, left_sm, right_sm, target_ref, w_any, l_any, r_any, out_ref,
+def kernel(sizes, whole_ref, w_any, l_any, r_any, out_ref,
            w_ref, l_refs, r_refs, table, table_sm, acc, s1, r1, s2, r2, s3, arr,
            sem_in, sem_s1, sem_r1, sem_s2, sem_r2, sem_s3, sem_r3):
     shards, classes, chunks, chunk, slots = sizes
@@ -62,11 +63,18 @@
     for u in range(pieces):
         span = pl.ds(u * part, part)
         pltpu.make_async_copy(w_any.at[span], w_ref.at[span], sem_in.at[2 * classes]).start()
-    for q in range(classes):
+
+    def fetch(q):
         for t in range(terms):
             pltpu.make_async_copy(l_any.at[q, t], l_refs[q].at[t], sem_in.at[q]).start()
             pltpu.make_async_copy(r_any.at[q, t], r_refs[q].at[t], sem_in.at[classes + q]).start()
 
+    def fetched(q):
+        pltpu.make_async_copy(l_any.at[q], l_refs[q], sem_in.at[q]).wait()
+        pltpu.make_async_copy(r_any.at[q], r_refs[q], sem_in.at[classes + q]).wait()
+
+    fetch(0)
+
     barrier = pltpu.get_barrier_semaphore()
     for other in (near_lo, near_hi):
         pl.semaphore_signal(barrier, inc=1, device_id={"op": other}, device_id_type=MESH)
@@ -76,7 +84,7 @@
         return carry
 
     lax.fori_loop(0, shards - 1, greet, 0)
-    fill_tables(target_ref, table, me, shards, slots)
+    fill_tables(whole_ref, classes, table, me, shards, slots)
     copy = pltpu.make_async_copy(table, table_sm, sem_in.at[2 * classes + 1])
     copy.start()
     copy.wait()
@@ -97,20 +105,16 @@
             recv_sem=sem_r3.at[q, me, part],
             device_id={"sec": peer(k)}, device_id_type=MESH)
 
-    def compute(i, q):
+    def compute(i, q, h):
         c = i // classes
-
-        @pl.when(jnp.int32(i) < classes)
-        def _():
-            pltpu.make_async_copy(l_any.at[q], l_refs[q], sem_in.at[q]).wait()
-            pltpu.make_async_copy(r_any.at[q], r_refs[q], sem_in.at[classes + q]).wait()
-
-        for start in range(0, chunk, BESIDE):
+        if q > 0 and h == 0:
+            pl.when(i == q)(functools.partial(fetched, q))
+        for start in range(h * half, (h + 1) * half, BESIDE):
             spots = []
-            for b in range(start, min(start + BESIDE, chunk)):
+            for b in range(start, min(start + BESIDE, (h + 1) * half)):
                 place_at = c * chunk + b
                 block = table_sm[q, peer(place_at // slots) * slots + place_at % slots]
-                spots.append((b, block, left_sm[block], right_sm[block]))
+                spots.append((b, block, table_sm[2 * classes, block], table_sm[2 * classes + 1, block]))
             mixes = []
             for b, block, left, right in spots:
                 mixed = jnp.dot(
@@ -125,13 +129,11 @@
             for (b, block, left, right), value in zip(spots, values):
                 acc[i, b] = value.reshape(acc.shape[2:])
 
-    def first(i):
+    def first(i, h):
         for j in range(2):
-            s1[0, i, :, j] = acc[i, 0:half, j * 2 + 1 - lo].astype(jnp.bfloat16)
-        first_copy(0, i).start()
-        for j in range(2):
-            s1[1, i, :, j] = acc[i, half:chunk, (1 - hi) * 2 + j].astype(jnp.bfloat16)
-        first_copy(1, i).start()
+            away = j * 2 + 1 - lo if h == 0 else (1 - hi) * 2 + j
+            s1[h, i, :, j] = acc[i, h * half:(h + 1) * half, away].astype(jnp.bfloat16)
+        first_copy(h, i).start()
 
     def second(i):
         first_copy(0, i).wait_recv()
@@ -166,9 +168,10 @@
     def step(i, carry):
         @pl.when(i < chunks)
         def _():
-            for q in range(classes):
-                pl.when((i % classes == q) & (i > 0))(functools.partial(compute, i, q))
-            first(i)
+            for h in range(2):
+                for q in range(classes):
+                    pl.when((i % classes == q) & (i + h > 0))(functools.partial(compute, i, q, h))
+                first(i, h)
 
         @pl.when((i >= LAG_SECOND) & (i < chunks + LAG_SECOND))
         def _():
@@ -180,7 +183,10 @@
 
         return carry
 
-    compute(0, 0)
+    fetched(0)
+    for q in range(1, classes):
+        fetch(q)
+    compute(0, 0, 0)
     pl.semaphore_wait(barrier, 2 + shards - 1)
     lax.fori_loop(0, chunks + LAG_ROUTE, step, 0)
 
@@ -235,14 +241,16 @@
     chunks = classes * blocks_here // chunk
     run = min(chunk, slots)
     half, rows, dests = chunk // 2, bl // parts, chunk // run
-    table = (2 * classes + -2 * classes % 8, blocks_here + -blocks_here % 128)
-    smem, vmem = pl.BlockSpec(memory_space=pltpu.SMEM), pl.BlockSpec(memory_space=pltpu.VMEM)
+    table = (2 * classes + 2 + (-2 * classes - 2) % 8, blocks_here + -blocks_here % 128)
+    vmem = pl.BlockSpec(memory_space=pltpu.VMEM)
+    sectors = jnp.pad(jnp.stack([left_sector, right_sector]), ((0, 0), (0, target.shape[1] - blocks_here)))
+    whole = jnp.concatenate([target, sectors], axis=0)
     wide, narrow = jnp.float32, jnp.bfloat16
     flops = 4 * blocks_here * classes * left_ops.shape[1] * bl * bl * br
     return pl.pallas_call(
         functools.partial(kernel, (shards, classes, chunks, chunk, slots)),
         out_shape=jax.ShapeDtypeStruct((blocks_here, rows, br), wide),
-        in_specs=[smem] * 2 + [vmem] + [pl.BlockSpec(memory_space=pl.ANY)] * 3,
+        in_specs=[vmem] + [pl.BlockSpec(memory_space=pl.ANY)] * 3,
         out_specs=vmem,
         scratch_shapes=[
             pltpu.VMEM(wavefunction.shape, wavefunction.dtype),
@@ -266,9 +274,9 @@
             pltpu.SemaphoreType.DMA((classes, shards, slots // run)),
         ],
         compiler_params=pltpu.CompilerParams(
-            collective_id=0, has_side_effects=True, vmem_limit_bytes=56 * 1024 * 1024),
+            collective_id=0, has_side_effects=True, vmem_limit_bytes=52 * 1024 * 1024),
         cost_estimate=pl.CostEstimate(flops=flops, bytes_accessed=8 * 1024 * 1024, transcendentals=0),
-    )(left_sector, right_sector, target, wavefunction, left_ops, right_ops)
+    )(whole, wavefunction, left_ops, right_ops)
 
 
 def solution(mesh):

time: 50.4 us -> 49.2 us (0.976)
  Pallas kernels: 47.9 us -> 46.4 us
  other arithmetic: 0 us -> 1.37 us
  local copies, waits for them, and re-layouts: 2.26 us -> 0.97 us
    pallas_call x1, Pallas kernels: 47.9 us -> 46.4 us  [per_device(): pl.pallas_call(functools.partial(kernel, (shards, classes, chunks, chunk,...]
    unnamed x1, local copies, waits for them, and re-layouts: 2.26 us -> 0.97 us
    concatenate x0 -> x1, other arithmetic: none -> 0.69 us  [per_device(): whole = jnp.concatenate([target, sectors], axis=0)]
    another operation x0 -> x1, other arithmetic: none -> 0.68 us  [per_device(): jnp.stack([left_sector, right_sector])]
where the time goes in v8:
time: 49.2 us; the launch traced here: 48.8 us
  Pallas kernels  46.4 us (94%)
  other arithmetic  1.37 us (3%)
  local copies, waits for them, and re-layouts  0.97 us (2%)
    pallas_call x1, Pallas kernels, per_device(): pl.pallas_call(functools.partial(kernel, (shards, classes, chunks, chunk,...  46.4 us

profile of v8, /device:TPU:0, one launch (start us, length us, event | category | flops | bytes accessed | tf_op | source)
XLA Modules:
  0.0 48.8 jit_solution(4575721702202988122)
XLA Ops:
  0.0 0.7 %pad_add_fusion.1 = s32[2,64]{1,0:T(2,128)S(1)} fusion(s32[1,64]{1,0:T(1,128)} %bitcast.2, s32[1,64]{1,0:T(1,128)} %bitcast.3), kind=kLoop, calls=%fused_computation.1 | loop fusion | flops 128 | bytes 1024 | tf_op jit(solution)/shard_map/stack | solution.py:246
  0.7 0.7 %pad_add_fusion.whole_ref = s32[4,512]{1,0:T(4,128)S(1)} fusion(s32[2,64]{1,0:T(2,128)S(1)} %pad_add_fusion.1, s32[2,512]{1,0:T(2,128)} %param.11), kind=kLoop, calls=%fused_computation | loop fusion | flops 2048 | bytes 12800 | tf_op jit(solution)/shard_map/concatenate | solution.py:247
  1.4 46.4 %shard_map.64 = f32[64,32,128]{2,1,0:T(8,128)S(1)} custom-call(s32[4,512]{1,0:T(4,128)S(1)} %pad_add_fusion.whole_ref, bf16[64,128,128]{2,1,0:T(8,128)(2,1)} %w_any.1, bf16[2,4,8,128,128]{4,3,2,1,0:T(8,128)(2,1)} %l_any.1, bf16[2,4,8,128,128]{4,3,2,1,0:T(8,128)(2,1)} %r_any.1), custom_call_target="tpu_custom_call" | custom-call | flops 4294967296 | bytes 8388608 | tf_op jit(solution)/shard_map/pallas_call | solution.py:250
  47.8 1.0 %copy.8 = f32[64,32,128]{2,1,0:T(8,128)} copy(f32[64,32,128]{2,1,0:T(8,128)S(1)} %shard_map.64) | data formatting | bytes 2097152

commit v9 on v8

--- a/solution.py
+++ b/solution.py
@@ -243,8 +243,10 @@
     half, rows, dests = chunk // 2, bl // parts, chunk // run
     table = (2 * classes + 2 + (-2 * classes - 2) % 8, blocks_here + -blocks_here % 128)
     vmem = pl.BlockSpec(memory_space=pltpu.VMEM)
-    sectors = jnp.pad(jnp.stack([left_sector, right_sector]), ((0, 0), (0, target.shape[1] - blocks_here)))
-    whole = jnp.concatenate([target, sectors], axis=0)
+    rest = target.shape[1] - blocks_here
+    whole = jnp.pad(target, ((0, 2), (0, 0)))
+    whole += jnp.pad(left_sector[None], ((classes, 1), (0, rest)))
+    whole += jnp.pad(right_sector[None], ((classes + 1, 0), (0, rest)))
     wide, narrow = jnp.float32, jnp.bfloat16
     flops = 4 * blocks_here * classes * left_ops.shape[1] * bl * bl * br
     return pl.pallas_call(

time: 49.2 us -> 48.5 us (0.986)
  other arithmetic: 1.37 us -> 0.73 us
    add x0 -> x1, other arithmetic: none -> 0.73 us  [per_device(): whole += jnp.pad(right_sector[None], ((classes + 1, 0), (0, rest)))]
    concatenate x1 -> x0, other arithmetic: 0.69 us -> none  [per_device(): whole = jnp.concatenate([target, sectors], axis=0)]
    another operation x1 -> x0, other arithmetic: 0.68 us -> none  [per_device(): jnp.stack([left_sector, right_sector])]
where the time goes in v9:
time: 48.5 us; the launch traced here: 48.1 us
  Pallas kernels  46.4 us (96%)
  local copies, waits for them, and re-layouts  0.97 us (2%)
  other arithmetic  0.73 us (2%)
    pallas_call x1, Pallas kernels, per_device(): pl.pallas_call(functools.partial(kernel, (shards, classes, chunks, chunk,...  46.4 us
    unnamed x1, local copies, waits for them, and re-layouts  0.97 us

profile of v9, /device:TPU:0, one launch (start us, length us, event | category | flops | bytes accessed | tf_op | source)
XLA Modules:
  0.0 48.1 jit_solution(7634444020026718266)
XLA Ops:
  0.0 0.7 %pad_add_fusion.whole_ref = s32[4,512]{1,0:T(4,128)S(1)} fusion(s32[1,64]{1,0:T(1,128)} %bitcast.2, s32[1,64]{1,0:T(1,128)} %bitcast.3, s32[2,512]{1,0:T(2,128)} %param.11), kind=kLoop, calls=%fused_computation | loop fusion | flops 4096 | bytes 12800 | tf_op jit(solution)/shard_map/add | solution.py:249
  0.7 46.4 %shard_map.64 = f32[64,32,128]{2,1,0:T(8,128)S(1)} custom-call(s32[4,512]{1,0:T(4,128)S(1)} %pad_add_fusion.whole_ref, bf16[64,128,128]{2,1,0:T(8,128)(2,1)} %w_any.1, bf16[2,4,8,128,128]{4,3,2,1,0:T(8,128)(2,1)} %l_any.1, bf16[2,4,8,128,128]{4,3,2,1,0:T(8,128)(2,1)} %r_any.1), custom_call_target="tpu_custom_call" | custom-call | flops 4294967296 | bytes 8388608 | tf_op jit(solution)/shard_map/pallas_call | solution.py:252
  47.2 1.0 %copy.8 = f32[64,32,128]{2,1,0:T(8,128)} copy(f32[64,32,128]{2,1,0:T(8,128)S(1)} %shard_map.64) | data formatting | bytes 2097152

commit v10 on v9

--- a/solution.py
+++ b/solution.py
@@ -166,20 +166,20 @@
                 arr[q, me, part] = share
 
     def step(i, carry):
+        @pl.when((i >= LAG_SECOND) & (i < chunks + LAG_SECOND))
+        def _():
+            second(i - LAG_SECOND)
+
+        @pl.when(i >= LAG_ROUTE)
+        def _():
+            route(i - LAG_ROUTE)
+
         @pl.when(i < chunks)
         def _():
             for h in range(2):
                 for q in range(classes):
                     pl.when((i % classes == q) & (i + h > 0))(functools.partial(compute, i, q, h))
                 first(i, h)
-
-        @pl.when((i >= LAG_SECOND) & (i < chunks + LAG_SECOND))
-        def _():
-            second(i - LAG_SECOND)
-
-        @pl.when(i >= LAG_ROUTE)
-        def _():
-            route(i - LAG_ROUTE)
 
         return carry
 

time: 48.5 us -> 49 us (1.010)
  Pallas kernels: 46.4 us -> 47.1 us
    pallas_call x1, Pallas kernels: 46.4 us -> 47.1 us  [per_device(): pl.pallas_call(functools.partial(kernel, (shards, classes, chunks, chunk,...]
where the time goes in v10:
time: 49 us; the launch traced here: 48.8 us
  Pallas kernels  47.1 us (96%)
  local copies, waits for them, and re-layouts  0.97 us (2%)
  other arithmetic  0.73 us (1%)
    pallas_call x1, Pallas kernels, per_device(): pl.pallas_call(functools.partial(kernel, (shards, classes, chunks, chunk,...  47.1 us

profile of v10, /device:TPU:0, one launch (start us, length us, event | category | flops | bytes accessed | tf_op | source)
XLA Modules:
  0.0 48.8 jit_solution(8379361835010387487)
XLA Ops:
  0.0 0.7 %pad_add_fusion.whole_ref = s32[4,512]{1,0:T(4,128)S(1)} fusion(s32[1,64]{1,0:T(1,128)} %bitcast.2, s32[1,64]{1,0:T(1,128)} %bitcast.3, s32[2,512]{1,0:T(2,128)} %param.11), kind=kLoop, calls=%fused_computation | loop fusion | flops 4096 | bytes 12800 | tf_op jit(solution)/shard_map/add | solution.py:249
  0.7 47.1 %shard_map.64 = f32[64,32,128]{2,1,0:T(8,128)S(1)} custom-call(s32[4,512]{1,0:T(4,128)S(1)} %pad_add_fusion.whole_ref, bf16[64,128,128]{2,1,0:T(8,128)(2,1)} %w_any.1, bf16[2,4,8,128,128]{4,3,2,1,0:T(8,128)(2,1)} %l_any.1, bf16[2,4,8,128,128]{4,3,2,1,0:T(8,128)(2,1)} %r_any.1), custom_call_target="tpu_custom_call" | custom-call | flops 4294967296 | bytes 8388608 | tf_op jit(solution)/shard_map/pallas_call | solution.py:252
  47.9 1.0 %copy.8 = f32[64,32,128]{2,1,0:T(8,128)} copy(f32[64,32,128]{2,1,0:T(8,128)S(1)} %shard_map.64) | data formatting | bytes 2097152
